TPU v7x, 512 devices: a whole 4x8x8 slice. The times are simulated.
512 devices in a mesh: row: 16 (over y_lo, x, core), col: 32 (over z, y_hi).
Axes of the slice: x: 4, y: 8 (y_hi: 4, y_lo: 2; y = y_hi * 2 + y_lo), z: 8, core: 2. Of those that a mesh axis runs over, the one named last changes fastest.
Arguments:
- panel_adjoint: float32 [24576, 512], P('row', 'col'), may hold values from -6 to 6
- panel_factor: float32 [24576, 512], P('row', 'col'), may hold values from -0.0390625 to 0.0390625
- diag_inverse: float32 [512, 512], P('row', 'col'), as said below
- head_factor: float32 [512, 8192], P('row', 'col'), may hold values from -0.25 to 0.25
- below_factor: float32 [24576, 8192], P('row', 'col'), may hold values from -0.0390625 to 0.0390625
- diag_adjoint: float32 [512, 512], P('row', 'col'), may hold values from -6 to 6
- head_adjoint: float32 [512, 8192], P('row', 'col'), may hold values from -6 to 6
- below_adjoint: float32 [24576, 8192], P('row', 'col'), may hold values from -6 to 6
Outputs:
- diag_updated: float32 [512, 512], P('row', 'col')
- head_updated: float32 [512, 8192], P('row', 'col')
- below_updated: float32 [24576, 8192], P('row', 'col')
Inputs may be any that keep to these rules, and one draw needn't show every extreme that they name: `diag_inverse`: upper triangular with a positive diagonal.
All inputs are finite; a program needn't handle non-finite values.
Results may differ from a plain program's by a relative error of at most 0.000084.
Values sent between devices are 32-bit elements; how exact they have to be, the bound alone decides.
No kernel may reach another device: no remote copies, remote signals or barrier semaphores. Data moves between devices by JAX's collectives and lax.ppermute only.
A program may use at most 64 MiB of HBM per device.

v0:
```python
import jax
import jax.numpy as jnp
from jax import lax
from jax.sharding import PartitionSpec as P


def mult(left, right):
    return jnp.dot(left, right, preferred_element_type=jnp.float32, precision=lax.Precision.HIGHEST)


def tmult(left, right):
    return lax.dot_general(
        left,
        right,
        (((0,), (0,)), ((), ())),
        preferred_element_type=jnp.float32,
        precision=lax.Precision.HIGHEST,
    )


def on_device(
    panel_adjoint,
    panel_factor,
    diag_inverse,
    head_factor,
    below_factor,
    diag_adjoint,
    head_adjoint,
    below_adjoint,
):
    inverse_part = lax.all_gather(diag_inverse, "row", axis=0, tiled=True)
    inverse_whole = lax.all_gather(inverse_part, "col", axis=1, tiled=True)
    panel_whole = lax.all_gather(panel_adjoint, "col", axis=1, tiled=True)
    solved = mult(panel_whole, inverse_whole)
    head_whole = lax.all_gather(head_factor, "row", axis=0, tiled=True)
    below_updated = below_adjoint - mult(solved, head_whole)
    head_term = lax.psum_scatter(
        tmult(solved, below_factor), "row", scatter_dimension=0, tiled=True
    )
    diag_term = lax.psum_scatter(
        tmult(solved, panel_factor), "row", scatter_dimension=0, tiled=True
    )
    diag_updated = diag_adjoint - diag_term
    head_updated = head_adjoint - head_term
    return (diag_updated, head_updated, below_updated)


def solution(mesh):
    placed = (
        P("row", "col"),
        P("row", "col"),
        P("row", "col"),
        P("row", "col"),
        P("row", "col"),
        P("row", "col"),
        P("row", "col"),
        P("row", "col"),
    )
    return jax.shard_map(
        on_device,
        mesh=mesh,
        in_specs=placed,
        out_specs=(P("row", "col"), P("row", "col"), P("row", "col")),
        check_vma=False,
    )
```

profile of v0, /device:TPU:16, one launch (start us, length us, event | category | flops | bytes accessed | tf_op | source)
XLA Modules:
  0.0 362.6 jit_solution(11307395783484746684)
XLA Ops:
  7.2 0.0 copy-start
  7.2 0.0 all-gather.6.cloned.1.call-start
  7.2 20.4 %all-gather = f32[16,32,16]{1,2,0:T(8,128)S(1)} all-gather(f32[1,32,16]{1,2,0:T(8,128)} %bitcast.12), channel_id=1, replica_groups=mesh['row'=16,'col'=32] {'row'}, dimensions={0}, use_global_device_ids=true | all-gather | bytes 34816 | tf_op jit(solution)/shard_map/all_gather | solution.py:31
  27.7 0.7 reshape.7
  28.4 0.0 all-gather.6.cloned.1.call-update
  28.4 0.0 all-gather.4.cloned.1.call-start
  28.5 0.7 all-gather.4.cloned.1.call-update
  29.2 0.0 copy-start.3
  29.2 0.0 reduce-scatter.7.cloned.1.call-start
  29.2 83.3 %all-gather.6.cloned.1.call-done = f32[512,512]{0,1:T(8,128)} async-done(((f32[512,16]{0,1:T(8,128)}), f32[512,512]{0,1:T(8,128)}) %all-gather.6.cloned.1.call-update) | async-done | bytes 1048592 | tf_op jit(solution)/shard_map/all_gather | solution.py:32
  112.6 93.1 %all-gather.4.cloned.1.call-done = f32[1536,512]{0,1:T(8,128)} async-done(((f32[1536,16]{0,1:T(8,128)}), f32[1536,512]{0,1:T(8,128)}) %all-gather.4.cloned.1.call-update) | async-done | bytes 3145744 | tf_op jit(solution)/shard_map/all_gather | solution.py:33
  205.7 12.5 %fusion = f32[1536,512]{1,0:T(8,128)S(1)} fusion(f32[1536,512]{0,1:T(8,128)} %all-gather.4.cloned.1.call-done, f32[512,512]{0,1:T(8,128)} %all-gather.6.cloned.1.call-done), kind=kOutput, calls=%fused_computation.1 | convolution fusion | flops 4831838208 | bytes 7340032 | tf_op jit(solution)/shard_map/dot_general | solution.py:8
  218.2 0.0 copy-start.1
  218.2 1.6 copy-done.1
  219.8 0.0 copy-done.3
  219.8 6.0 %fusion.1 = f32[512,16]{1,0:T(8,128)} fusion(f32[1536,512]{1,0:T(8,128)S(1)} %fusion, f32[1536,16]{0,1:T(8,128)S(1)} %copy-done.3), kind=kOutput, calls=%fused_computation.2 | convolution fusion | flops 150994944 | bytes 3276800
  225.8 0.0 reduce-scatter.7.cloned.1.call-update
  225.8 0.0 copy-start.2
  225.8 0.0 reduce-scatter.5.cloned.1.call-start
  225.9 0.0 copy-done
  225.9 7.9 %fusion.2 = f32[512,256]{1,0:T(8,128)} fusion(f32[1536,512]{1,0:T(8,128)} %copy-done.1, f32[1536,256]{1,0:T(8,128)S(1)} %copy-done), kind=kOutput, calls=%fused_computation.3 | convolution fusion | flops 2415919104 | bytes 5242880 | tf_op jit(solution)/shard_map/dot_general | solution.py:12
  233.7 0.0 reduce-scatter.5.cloned.1.call-update
  233.8 0.0 copy-done.4
  233.8 18.9 %all_gather.15 = f32[512,256]{1,0:T(8,128)S(1)} all-gather(f32[32,256]{1,0:T(8,128)S(1)} %copy-done.4), channel_id=1, replica_groups=mesh['row'=16,'col'=32] {'row'}, dimensions={0}, use_global_device_ids=true | all-gather | bytes 557056 | tf_op jit(solution)/shard_map/all_gather | solution.py:35
  252.6 0.0 copy-done.2
  252.6 5.7 %convolution_subtract_fusion = f32[1536,256]{1,0:T(8,128)} fusion(f32[1536,256]{1,0:T(8,128)S(1)} %copy-done.2, f32[1536,512]{1,0:T(8,128)} %copy-done.1, f32[512,256]{1,0:T(8,128)S(1)} %all_gather.15), kind=kOutput, calls=%fused_computation | convolution fusion | flops 2416312320 | bytes 6815744 | tf_op jit(solution)/shard_map/dot_general | solution.py:8
  258.3 29.6 %reduce-scatter.7.cloned.1.call-done = f32[32,16]{1,0:T(8,128)} async-done(((f32[512,16]{1,0:T(8,128)}), f32[32,16]{1,0:T(8,128)}) %reduce-scatter.7.cloned.1.call-update) | async-done | bytes 2064
  288.0 0.8 copy.14
  288.8 0.0 copy-done.6
  288.8 0.6 sub.9
  289.4 65.3 %reduce-scatter.5.cloned.1.call-done = f32[32,256]{1,0:T(8,128)} async-done(((f32[512,256]{1,0:T(8,128)}), f32[32,256]{1,0:T(8,128)}) %reduce-scatter.5.cloned.1.call-update) | async-done | bytes 32784 | tf_op jit(solution)/shard_map/reduce_scatter | solution.py:37
  354.7 1.4 sub.10
  (5 shorter events, 0.1 us)
Async XLA Ops:
  7.2 218.7 %copy-start = (f32[1536,256]{1,0:T(8,128)S(1)}, f32[1536,256]{1,0:T(8,128)}, u32[]{:S(2)}) copy-start(f32[1536,256]{1,0:T(8,128)} %param.12) | copy-start | bytes 4718596
  7.2 105.4 %all-gather.6.cloned.1.call-start = ((), (), s32[]{:S(2)}) async-start(), calls=%async_computation.3 | async-start | bytes 1081344 | tf_op jit(solution)/shard_map/all_gather | solution.py:32
  28.4 177.2 %all-gather.4.cloned.1.call-start = ((), (), s32[]{:S(2)}) async-start(), calls=%async_computation.2 | async-start | bytes 3244032 | tf_op jit(solution)/shard_map/all_gather | solution.py:33
  29.2 190.6 %copy-start.3 = (f32[1536,16]{0,1:T(8,128)S(1)}, f32[1536,16]{0,1:T(8,128)}, u32[]{:S(2)}) copy-start(f32[1536,16]{0,1:T(8,128)} %param.9) | copy-start | bytes 294916
  29.2 258.8 %reduce-scatter.7.cloned.1.call-start = ((), (), s32[]{:S(2)}) async-start(), calls=%async_computation.5 | async-start | bytes 278528
  218.2 1.6 copy-start.1
  225.8 8.0 %copy-start.4 = (f32[32,256]{1,0:T(8,128)S(1)}, f32[32,256]{1,0:T(8,128)}, u32[]{:S(2)}) copy-start(f32[32,256]{1,0:T(8,128)} %param.11) | copy-start | bytes 98308
  225.8 26.8 %copy-start.2 = (f32[1536,256]{1,0:T(8,128)S(1)}, f32[1536,256]{1,0:T(8,128)}, u32[]{:S(2)}) copy-start(f32[1536,256]{1,0:T(8,128)} %param.15) | copy-start | bytes 4718596
  225.8 128.9 %reduce-scatter.5.cloned.1.call-start = ((), (), s32[]{:S(2)}) async-start(), calls=%async_computation.4 | async-start | bytes 557056 | tf_op jit(solution)/shard_map/reduce_scatter | solution.py:37
  252.6 36.1 %copy-start.6 = (f32[32,16]{0,1:T(8,128)S(1)}, f32[32,16]{0,1:T(8,128)}, u32[]{:S(2)}) copy-start(f32[32,16]{0,1:T(8,128)} %param.13) | copy-start | bytes 6148
  252.6 102.0 %copy-start.5 = (f32[32,256]{1,0:T(8,128)S(1)}, f32[32,256]{1,0:T(8,128)}, u32[]{:S(2)}) copy-start(f32[32,256]{1,0:T(8,128)} %param.14) | copy-start | bytes 98308
Sparse Core Ops, SparseCore 0:
  28.6 83.9 all-gather.5
  115.8 89.8 all-gather.3
  225.9 62.0 reduce-scatter.6
  290.9 63.7 reduce-scatter.4
where the time goes:
time: 363 us
  waiting for transfers between devices  272 us (75%)
  blocking collectives  39.3 us (11%)
  matrix products  32 us (9%)
  between operations  13.8 us (4%)
    all_gather x1, waiting for transfers between devices, on_device(): panel_whole = lax.all_gather(panel_adjoint, 'col', axis=1, tiled=True)  93.1 us
    all_gather x1, waiting for transfers between devices, on_device(): inverse_whole = lax.all_gather(inverse_part, 'col', axis=1, tiled=True)  83.3 us
    reduce_scatter x1, waiting for transfers between devices, on_device(): lax.psum_scatter(tmult(solved, below_factor), 'row', scatter_dimension=0,...  65.3 us
    unnamed x5, waiting for transfers between devices  30.4 us
    all_gather x1, blocking collectives, on_device(): inverse_part = lax.all_gather(diag_inverse, 'row', axis=0, tiled=True)  20.4 us
    all_gather x1, blocking collectives, on_device(): head_whole = lax.all_gather(head_factor, 'row', axis=0, tiled=True)  18.9 us
    dot_general x2, matrix products, mult(): jnp.dot(left, right, preferred_element_type=jnp.float32, precision=lax.Pr...  18.2 us
    dot_general x1, matrix products, tmult(): lax.dot_general(left, right, (((0,), (0,)), ((), ())), preferred_element_...  7.85 us
  transfers between devices with their start and end apart: 4, of which 4 were waited for; matrix products, arithmetic and copies ran while one was open for 4% of the time, Pallas kernels for 0%

commit v1 on v0

--- a/solution.py
+++ b/solution.py
@@ -29,8 +29,13 @@
     below_adjoint,
 ):
     inverse_part = lax.all_gather(diag_inverse, "row", axis=0, tiled=True)
-    inverse_whole = lax.all_gather(inverse_part, "col", axis=1, tiled=True)
-    panel_whole = lax.all_gather(panel_adjoint, "col", axis=1, tiled=True)
+    inverse_whole, panel_whole = jnp.split(
+        lax.all_gather(
+            jnp.concatenate([inverse_part, panel_adjoint], axis=0), "col", axis=1, tiled=True
+        ),
+        [inverse_part.shape[0]],
+        axis=0,
+    )
     solved = mult(panel_whole, inverse_whole)
     head_whole = lax.all_gather(head_factor, "row", axis=0, tiled=True)
     below_updated = below_adjoint - mult(solved, head_whole)

time: 363 us -> 291 us (0.80)
  waiting for transfers between devices: 272 us -> 195 us
  blocking collectives: 39.3 us -> 43.1 us
    all_gather x2 -> x1, waiting for transfers between devices: 176 us -> 102 us  [on_device(): lax.all_gather(jnp.concatenate([inverse_part, panel_adjoint], axis=0), 'c...]
    all_gather x1, blocking collectives: 18.9 us -> 22.7 us  [on_device(): head_whole = lax.all_gather(head_factor, 'row', axis=0, tiled=True)]
    unnamed x5 -> x4, waiting for transfers between devices: 30.4 us -> 26.8 us
  transfers between devices with their start and end apart: 4 -> 3, of which waited for: 4 -> 3; matrix products, arithmetic and copies ran while one was open for 4% -> 5% of each run, Pallas kernels for 0% -> 0%
where the time goes in v1:
time: 291 us; the launch traced here: 290 us
  waiting for transfers between devices  195 us (67%)
  blocking collectives  43.1 us (15%)
  matrix products  32 us (11%)
  between operations  13.8 us (5%)
  other arithmetic  3.54 us (1%)
    all_gather x1, waiting for transfers between devices, on_device(): lax.all_gather(jnp.concatenate([inverse_part, panel_adjoint], axis=0), 'c...  102 us
    reduce_scatter x1, waiting for transfers between devices, on_device(): lax.psum_scatter(tmult(solved, below_factor), 'row', scatter_dimension=0,...  65.9 us
    unnamed x4, waiting for transfers between devices  26.8 us
    all_gather x1, blocking collectives, on_device(): head_whole = lax.all_gather(head_factor, 'row', axis=0, tiled=True)  22.7 us
    all_gather x1, blocking collectives, on_device(): inverse_part = lax.all_gather(diag_inverse, 'row', axis=0, tiled=True)  20.4 us
    dot_general x2, matrix products, mult(): jnp.dot(left, right, preferred_element_type=jnp.float32, precision=lax.Pr...  18.2 us
    dot_general x1, matrix products, tmult(): lax.dot_general(left, right, (((0,), (0,)), ((), ())), preferred_element_...  7.85 us
    unnamed x1, matrix products  5.97 us
  transfers between devices with their start and end apart: 3, of which 3 were waited for; matrix products, arithmetic and copies ran while one was open for 5% of the time, Pallas kernels for 0%

profile of v1, /device:TPU:16, one launch (start us, length us, event | category | flops | bytes accessed | tf_op | source)
XLA Modules:
  0.0 290.3 jit_solution(16173304501996463588)
XLA Ops:
  7.2 0.0 copy-start
  7.2 0.0 all-gather.3.cloned.1.call-start
  7.2 20.4 %all-gather = f32[16,32,16]{1,2,0:T(8,128)S(1)} all-gather(f32[1,32,16]{1,2,0:T(8,128)} %bitcast.10), channel_id=1, replica_groups=mesh['row'=16,'col'=32] {'row'}, dimensions={0}, use_global_device_ids=true | all-gather | bytes 34816 | tf_op jit(solution)/shard_map/all_gather | solution.py:31
  27.7 0.1 reshape.7
  27.8 1.6 pad_maximum_fusion
  29.4 0.0 all-gather.3.cloned.1.call-update
  29.4 0.0 copy-start.3
  29.4 0.0 reduce-scatter.7.cloned.1.call-start
  29.4 102.4 %all-gather.3.cloned.1.call-done = f32[2048,512]{0,1:T(8,128)} async-done(((f32[2048,16]{0,1:T(8,128)}), f32[2048,512]{0,1:T(8,128)}) %all-gather.3.cloned.1.call-update) | async-done | bytes 4194320 | tf_op jit(solution)/shard_map/all_gather | solution.py:33
  131.8 12.5 %fusion = f32[1536,512]{1,0:T(8,128)S(1)} fusion(f32[2048,512]{0,1:T(8,128)} %all-gather.3.cloned.1.call-done), kind=kOutput, calls=%fused_computation | convolution fusion | flops 4831838208 | bytes 7340032 | tf_op jit(solution)/shard_map/dot_general | solution.py:8
  144.3 0.0 copy-start.1
  144.3 1.6 copy-done.1
  145.9 0.0 copy-done.3
  145.9 6.0 %fusion.3 = f32[512,16]{1,0:T(8,128)} fusion(f32[1536,512]{1,0:T(8,128)S(1)} %fusion, f32[1536,16]{0,1:T(8,128)S(1)} %copy-done.3), kind=kOutput, calls=%fused_computation.5 | convolution fusion | flops 150994944 | bytes 3276800
  151.9 0.0 copy-start.4
  151.9 0.0 reduce-scatter.7.cloned.1.call-update
  151.9 0.0 copy-start.2
  152.0 0.0 reduce-scatter.5.cloned.1.call-start
  152.0 0.0 copy-done
  152.0 7.8 %fusion.4 = f32[512,256]{1,0:T(8,128)} fusion(f32[1536,512]{1,0:T(8,128)} %copy-done.1, f32[1536,256]{1,0:T(8,128)S(1)} %copy-done), kind=kOutput, calls=%fused_computation.6 | convolution fusion | flops 2415919104 | bytes 5242880 | tf_op jit(solution)/shard_map/dot_general | solution.py:12
  159.9 0.0 reduce-scatter.5.cloned.1.call-update
  159.9 0.0 copy-done.4
  159.9 22.7 %all_gather.11 = f32[512,256]{1,0:T(8,128)S(1)} all-gather(f32[32,256]{1,0:T(8,128)S(1)} %copy-done.4), channel_id=1, replica_groups=mesh['row'=16,'col'=32] {'row'}, dimensions={0}, use_global_device_ids=true | all-gather | bytes 557056 | tf_op jit(solution)/shard_map/all_gather | solution.py:40
  182.6 0.0 copy-done.2
  182.6 5.7 %convolution_subtract_fusion = f32[1536,256]{1,0:T(8,128)} fusion(f32[1536,256]{1,0:T(8,128)S(1)} %copy-done.2, f32[1536,512]{1,0:T(8,128)} %copy-done.1, f32[512,256]{1,0:T(8,128)S(1)} %all_gather.11), kind=kOutput, calls=%fused_computation.2 | convolution fusion | flops 2416312320 | bytes 6815744 | tf_op jit(solution)/shard_map/dot_general | solution.py:8
  188.3 26.8 %reduce-scatter.7.cloned.1.call-done = f32[32,16]{1,0:T(8,128)} async-done(((f32[512,16]{1,0:T(8,128)}), f32[32,16]{1,0:T(8,128)}) %reduce-scatter.7.cloned.1.call-update) | async-done | bytes 2064
  215.1 0.8 copy.14
  215.9 0.0 copy-done.6
  215.9 0.6 sub.9
  216.5 65.9 %reduce-scatter.5.cloned.1.call-done = f32[32,256]{1,0:T(8,128)} async-done(((f32[512,256]{1,0:T(8,128)}), f32[32,256]{1,0:T(8,128)}) %reduce-scatter.5.cloned.1.call-update) | async-done | bytes 32784 | tf_op jit(solution)/shard_map/reduce_scatter | solution.py:42
  282.4 0.0 copy-done.5
  282.4 1.4 sub.10
  (3 shorter events, 0.0 us)
Async XLA Ops:
  7.2 144.8 %copy-start = (f32[1536,256]{1,0:T(8,128)S(1)}, f32[1536,256]{1,0:T(8,128)}, u32[]{:S(2)}) copy-start(f32[1536,256]{1,0:T(8,128)} %param.12) | copy-start | bytes 4718596
  7.2 124.6 %all-gather.3.cloned.1.call-start = ((), (), s32[]{:S(2)}) async-start(), calls=%async_computation.2 | async-start | bytes 4325376 | tf_op jit(solution)/shard_map/all_gather | solution.py:33
  29.4 116.6 %copy-start.3 = (f32[1536,16]{0,1:T(8,128)S(1)}, f32[1536,16]{0,1:T(8,128)}, u32[]{:S(2)}) copy-start(f32[1536,16]{0,1:T(8,128)} %param.9) | copy-start | bytes 294916
  29.4 185.7 %reduce-scatter.7.cloned.1.call-start = ((), (), s32[]{:S(2)}) async-start(), calls=%async_computation.4 | async-start | bytes 278528
  144.3 1.6 copy-start.1
  151.9 8.0 %copy-start.4 = (f32[32,256]{1,0:T(8,128)S(1)}, f32[32,256]{1,0:T(8,128)}, u32[]{:S(2)}) copy-start(f32[32,256]{1,0:T(8,128)} %param.11) | copy-start | bytes 98308
  151.9 30.7 %copy-start.2 = (f32[1536,256]{1,0:T(8,128)S(1)}, f32[1536,256]{1,0:T(8,128)}, u32[]{:S(2)}) copy-start(f32[1536,256]{1,0:T(8,128)} %param.15) | copy-start | bytes 4718596
  152.0 130.4 %reduce-scatter.5.cloned.1.call-start = ((), (), s32[]{:S(2)}) async-start(), calls=%async_computation.3 | async-start | bytes 557056 | tf_op jit(solution)/shard_map/reduce_scatter | solution.py:42
  182.6 33.3 %copy-start.6 = (f32[32,16]{0,1:T(8,128)S(1)}, f32[32,16]{0,1:T(8,128)}, u32[]{:S(2)}) copy-start(f32[32,16]{0,1:T(8,128)} %param.13) | copy-start | bytes 6148
  182.6 99.8 %copy-start.5 = (f32[32,256]{1,0:T(8,128)S(1)}, f32[32,256]{1,0:T(8,128)}, u32[]{:S(2)}) copy-start(f32[32,256]{1,0:T(8,128)} %param.14) | copy-start | bytes 98308
Sparse Core Ops, SparseCore 0:
  29.5 102.2 all-gather.2
  152.1 63.0 reduce-scatter.6
  218.2 64.2 reduce-scatter.4
